TPU v7x, 32 devices: a whole 2x2x4 slice. The times are simulated.
32 devices in a mesh: row: 8 (over y, x, core), col: 4 (over z).
Axes of the slice: x: 2, y: 2, z: 4, core: 2. Of those that a mesh axis runs over, the one named last changes fastest.
Arguments:
- source_v: float32 [2, 4, 2560, 768], P(None, 'col', 'row'), may hold values from -6 to 6
- source_omega: float32 [2, 4, 2560, 768], P(None, 'col', 'row'), may hold values from -6 to 6
- forward_map: float32 [768, 768], P('col'), may hold values from -0.21875 to 0.21875
- back_maps: float32 [2, 768, 768], P(None, 'col'), may hold values from -0.21875 to 0.21875
- eigenvalues: float32 [768], replicated, may hold values from 0.02 to 4
- penalty: float32 [768, 3840], P('row'), may hold values from 0.05 to 4
Outputs:
- v_field: float32 [2, 4, 2560, 768], P(None, 'col', 'row')
- omega_field: float32 [2, 4, 2560, 768], P(None, 'col', 'row')
All inputs are finite; a program needn't handle non-finite values.
Results may differ from a plain program's by a relative error of at most 0.000098.
Values sent between devices are 32-bit elements; how exact they have to be, the bound alone decides.
A program may use at most 128 MiB of HBM per device.

v0:
```python
import math
import jax
import jax.numpy as jnp
from jax import lax
from jax.sharding import PartitionSpec as P


def helm_scale(eigen_part, flow_wave, span_wave):
    return 1.0 / (1.0 + eigen_part + 0.05 * (flow_wave * flow_wave + span_wave * span_wave))


def form_velocity(flow_wave, span_wave, derivative, vorticity):
    wave_sq = jnp.maximum(flow_wave * flow_wave + span_wave * span_wave, 1.0)
    along_real = (span_wave * vorticity[1] - flow_wave * derivative[1]) / wave_sq
    along_imag = (flow_wave * derivative[0] - span_wave * vorticity[0]) / wave_sq
    across_real = -(span_wave * derivative[1] + flow_wave * vorticity[1]) / wave_sq
    across_imag = (span_wave * derivative[0] + flow_wave * vorticity[0]) / wave_sq
    return (jnp.stack([along_real, along_imag]), jnp.stack([across_real, across_imag]))


def form_vorticity(flow_wave, span_wave, along, across):
    real_part = flow_wave * across[1] - span_wave * along[1]
    imag_part = span_wave * along[0] - flow_wave * across[0]
    return jnp.stack([real_part, imag_part])


def spanwise_tables(blocks_k, blocks_z, count_z):
    coarse_k = jnp.arange(blocks_k, dtype=jnp.int32)
    coarse_k = jnp.where(coarse_k < blocks_k // 2, coarse_k, coarse_k + blocks_z - blocks_k)
    coarse_z = jnp.arange(blocks_z, dtype=jnp.int32)
    fine_index = jnp.arange(128, dtype=jnp.int32)
    coarse_angle = (
        2.0
        * math.pi
        / blocks_z
        * (coarse_z[:, None] * coarse_k[None, :] % blocks_z).astype(jnp.float32)
    )
    twist_angle = (
        2.0
        * math.pi
        / count_z
        * (coarse_z[:, None] * fine_index[None, :] % count_z).astype(jnp.float32)
    )
    fine_angle = (
        2.0 * math.pi / 128 * (fine_index[:, None] * fine_index[None, :] % 128).astype(jnp.float32)
    )
    return (coarse_angle, twist_angle, fine_angle)


def block_table(cos_part, sin_part, axis_in):
    first = jnp.stack([cos_part, -sin_part], axis=axis_in)
    second = jnp.stack([sin_part, cos_part], axis=axis_in)
    return jnp.stack([first, second], axis=0)


def twist_apply(data, twist_cos, twist_sin):
    real_part = data[:, 0]
    imag_part = data[:, 1]
    return jnp.stack(
        [
            real_part * twist_cos - imag_part * twist_sin,
            real_part * twist_sin + imag_part * twist_cos,
        ],
        axis=1,
    )


def spanwise_pass(spanwise, factor_grid, count_z):
    count_kz = spanwise.shape[-1]
    blocks_k = count_kz // 128
    blocks_z = count_z // 128
    lead = spanwise.shape[:4]
    data = spanwise.reshape(lead + (blocks_k, 128))
    coarse_angle, twist_angle, fine_angle = spanwise_tables(blocks_k, blocks_z, count_z)
    coarse_cos, coarse_sin = (jnp.cos(coarse_angle), jnp.sin(coarse_angle))
    twist_cos, twist_sin = (jnp.cos(twist_angle), jnp.sin(twist_angle))
    fine_cos, fine_sin = (jnp.cos(fine_angle), jnp.sin(fine_angle))
    coarse_fwd = block_table(coarse_cos, coarse_sin, 1)
    fine_fwd = block_table(fine_cos, fine_sin, 1)
    fine_inv = block_table(fine_cos, -fine_sin, 1)
    coarse_inv = jnp.transpose(block_table(coarse_cos, -coarse_sin, 1), (0, 2, 1, 3)) / count_z
    data = jnp.einsum("cadk,fdxyks->fcxyas", coarse_fwd, data, precision=lax.Precision.HIGHEST)
    data = twist_apply(data, twist_cos, twist_sin)
    data = jnp.einsum("cnds,fdxyas->fcxyan", fine_fwd, data, precision=lax.Precision.HIGHEST)
    data = data * factor_grid
    data = jnp.einsum("ckdn,fdxyan->fcxyak", fine_inv, data, precision=lax.Precision.HIGHEST)
    data = twist_apply(data, twist_cos, -twist_sin)
    data = jnp.einsum("cdak,fdxyas->fcxyks", coarse_inv, data, precision=lax.Precision.HIGHEST)
    return data.reshape(lead + (count_kz,))


def shards(source_v, source_omega, forward_map, back_maps, eigenvalues, penalty):
    local_kx = source_v.shape[1]
    local_kz = source_v.shape[2]
    count_kz = local_kz * lax.axis_size("row")
    half_kz = count_kz // 2
    local_y = penalty.shape[0]
    count_z = penalty.shape[1]
    flow_index = lax.axis_index("col") * local_kx + jnp.arange(local_kx, dtype=jnp.int32)
    flow_wave = 0.5 * flow_index.astype(jnp.float32)
    span_index = lax.axis_index("row") * local_kz + jnp.arange(local_kz, dtype=jnp.int32)
    span_local = (
        jnp.where(span_index < half_kz, span_index, span_index - count_kz).astype(jnp.float32)
        * 8.0
        / half_kz
    )
    scaling = helm_scale(
        eigenvalues[None, None, :], flow_wave[:, None, None], span_local[None, :, None]
    )
    sources = jnp.stack([source_v, source_omega])
    flow_column = flow_wave[:, None, None]
    span_row = span_local[None, None, :]
    partial_coeffs = jnp.einsum(
        "fcxkn,jn->fcxkj",
        sources,
        lax.all_gather(forward_map, "col", axis=0, tiled=True),
        precision=lax.Precision.HIGHEST,
    )
    coeffs = partial_coeffs * scaling
    block_rows = lax.all_gather(back_maps, "col", axis=1, tiled=True)
    values = jnp.einsum("yj,fcxkj->fcxyk", block_rows[0], coeffs, precision=lax.Precision.HIGHEST)
    derivative = jnp.einsum(
        "yj,cxkj->cxyk", block_rows[1], coeffs[0], precision=lax.Precision.HIGHEST
    )
    along, across = form_velocity(flow_column, span_row, derivative, values[1])
    fields = jnp.stack([along, values[0], across])
    spanwise = lax.all_to_all(fields, "row", split_axis=3, concat_axis=4, tiled=True)
    factor_grid = jnp.transpose(
        (1.0 / (1.0 + penalty)).reshape(local_y, 128, count_z // 128), (0, 2, 1)
    )
    result = spanwise_pass(spanwise, factor_grid, count_z)
    returned = lax.all_to_all(result, "row", split_axis=4, concat_axis=3, tiled=True)
    v_part = returned[1]
    omega_part = form_vorticity(flow_column, span_row, returned[0], returned[2])
    return (jnp.transpose(v_part, (0, 1, 3, 2)), jnp.transpose(omega_part, (0, 1, 3, 2)))


def solution(mesh):
    placed = (
        P(None, "col", "row", None),
        P(None, "col", "row", None),
        P("col", None),
        P(None, "col", None),
        P(),
        P("row", None),
    )
    return jax.shard_map(
        shards,
        mesh=mesh,
        in_specs=placed,
        out_specs=(P(None, "col", "row", None), P(None, "col", "row", None)),
        check_vma=False,
    )
```

profile of v0, /device:TPU:0, one launch (start us, length us, event | category | flops | bytes accessed | tf_op | source)
XLA Modules:
  0.0 500.1 jit_solution(2554494599906409312)
XLA Ops:
  9.6 53.2 %all-gather.3.cloned.1.call-done = f32[768,768]{1,0:T(8,128)} async-done(((f32[192,768]{1,0:T(8,128)}), f32[768,768]{1,0:T(8,128)}) %all-gather.3.cloned.1.call-update) | async-done | bytes 2359312 | tf_op jit(solution)/shard_map/all_gather | solution.py:116
  62.8 13.7 %fusion.23 = f32[2,2,320,768]{3,2,1,0:T(8,128)} fusion(f32[768,768]{1,0:T(8,128)} %all-gather.3.cloned.1.call-done, f32[1,2,1,320,768]{4,3,1,0,2:T(8,128)} %bitcast.194, f32[1,2,1,320,768]{4,3,1,0,2:T(8,128)} %bitcast.195, f32[320,768]{1,0:T(8,128)S(1)} %add_divide_fusion.2), kind=kOutput, calls=%fused_computation.31 | convolution fusion | flops 9061662720 | bytes 11206656 | tf_op jit(solution)/shard_map/fcxkn,jn->fcxkj/dot_general | solution.py:113
  76.5 76.1 %all-gather.5.cloned.1.call-done = f32[2,768,768]{2,1,0:T(8,128)} async-done(((f32[2,192,768]{2,1,0:T(8,128)}), f32[2,768,768]{2,1,0:T(8,128)}) %all-gather.5.cloned.1.call-update) | async-done | bytes 4718608 | tf_op jit(solution)/shard_map/all_gather | solution.py:120
  152.6 13.3 %fusion.21 = f32[2,2,320,768]{3,2,1,0:T(8,128)S(1)} fusion(f32[2,2,320,768]{3,2,1,0:T(8,128)} %fusion.23, f32[2,768,768]{2,1,0:T(8,128)} %all-gather.5.cloned.1.call-done), kind=kOutput, calls=%fused_computation.29 | convolution fusion | flops 9059696640 | bytes 10223616 | tf_op jit(solution)/shard_map/yj,fcxkj->fcxyk/dot_general | solution.py:121
  166.0 5.5 %fusion.26 = f32[2,1,768,320]{2,3,0,1:T(8,128)S(1)} fusion(f32[2,768,768]{2,1,0:T(8,128)S(1)} %copy-done.2, f32[2,2,320,768]{3,2,1,0:T(8,128)S(1)} %copy-done), kind=kOutput, calls=%fused_computation.36 | convolution fusion | flops 4529848320 | bytes 6291456 | tf_op jit(solution)/shard_map/yj,cxkj->cxyk/dot_general | solution.py:122
  172.5 2.9 pad_maximum_fusion
  175.5 13.2 %copy.41 = f32[3,2,1,768,320]{4,1,0,2,3:T(2,128)} copy(f32[3,2,1,768,320]{3,4,1,0,2:T(8,128)} %pad_maximum_fusion) | data formatting | bytes 11796480 | tf_op jit(solution)/shard_map/stack | solution.py:126
  188.7 5.0 all-to-all-start
  197.2 1.8 copy.47
  201.7 71.9 %all-to-all-done = f32[3,2,1,768,320]{4,1,0,2,3:T(2,128)} async-done(((f32[3,2,1,768,320]{4,1,0,2,3:T(2,128)}), f32[3,2,1,768,320]{4,1,0,2,3:T(2,128)}, u32[]{:S(2)}, u32[]{:S(2)}) %all-to-all-start) | async-done | bytes 5898272 | tf_op jit(solution)/shard_map/all_to_all | solution.py:127
  273.7 3.5 copy.42
  277.1 7.0 %copy.77 = f32[3,2,1,96,8,320]{5,4,1,3,0,2:T(8,128)} copy(f32[3,2,1,96,8,320]{5,3,4,1,0,2:T(8,128)S(1)} %bitcast.185) | data formatting | bytes 11796480 | tf_op jit(solution)/shard_map/reshape.27
  284.1 9.5 %reshape.764 = f32[3,2,96,20,128,1]{4,3,1,2,0,5:T(8,128)} reshape(f32[3,2,1,96,8,320]{5,4,1,3,0,2:T(8,128)} %copy.77) | data formatting | bytes 11796480 | tf_op jit(solution)/shard_map/reshape.27
  293.6 10.7 %fusion.13 = f32[3,2,1,96,30,128]{5,4,1,3,0,2:T(8,128)S(1)} fusion(f32[3,2,96,20,128,1]{4,3,1,2,0,5:T(8,128)} %reshape.764, f32[1,30,2,20]{1,3,2,0:T(8,128)S(1)} %get-tuple-element.27, f32[1,30,2,20]{1,3,2,0:T(8,128)S(1)} %get-tuple-element.30), kind=kOutput, calls=%fused_computation.23 | convolution fusion | flops 1061685632 | bytes 14755200 | tf_op jit(solution)/shard_map/cadk,fdxyks->fcxyas/dot_general | solution.py:82
  304.3 2.5 multiply_subtract_fusion.1
  308.3 13.7 %fusion.5 = f32[3,96,30,2,128,1]{4,1,5,3,2,0:T(8,128)S(1)} fusion(f32[3,2,96,30,128,1]{4,3,1,2,0,5:T(8,128)S(1)} %maximum_bitcast_fusion, f32[1,128,2,128]{3,1,2,0:T(8,128)S(1)} %get-tuple-element.21, f32[1,128,2,128]{3,1,2,0:T(8,128)S(1)} %get-tuple-element.24), kind=kOutput, calls=%fused_computation.9 | convolution fusion | flops 6794838016 | bytes 17956864 | tf_op jit(solution)/shard_map/cnds,fdxyas->fcxyan/dot_general | solution.py:84
  322.1 7.6 %fusion.16 = f32[3,96,30,2,128]{4,1,3,2,0:T(8,128)S(1)} fusion(f32[3,96,30,2,128,1]{4,1,5,3,2,0:T(8,128)S(1)} %fusion.5, f32[96,30,128]{2,0,1:T(8,128)S(1)} %copy-done.1, f32[1,128,2,128]{3,1,2,0:T(8,128)S(1)} %get-tuple-element.25, f32[1,128,2,128]{3,1,2,0:T(8,128)S(1)} %get-tuple-element.20), kind=kOutput, calls=%fused_computation.24 | convolution fusion | flops 6797049856 | bytes 19431424 | tf_op jit(solution)/shard_map/ckdn,fdxyan->fcxyak/dot_general | solution.py:86
  329.7 5.4 %copy.88 = f32[3,96,30,2,128]{4,2,3,1,0:T(8,128)S(1)} copy(f32[3,96,30,2,128]{4,1,3,2,0:T(8,128)S(1)} %fusion.16) | data formatting | bytes 17694720 | tf_op jit(solution)/shard_map/ckdn,fdxyan->fcxyak/dot_general | solution.py:86
  336.9 10.1 %fusion.19 = f32[3,2,1,96,20,128]{5,4,1,3,0,2:T(8,128)} fusion(f32[3,1,1,96,30,128]{5,4,1,3,0,2:T(8,128)S(1)} %get-tuple-element.9, f32[3,1,1,96,30,128]{5,4,1,3,0,2:T(8,128)S(1)} %get-tuple-element.8, f32[1,30,2,20]{1,3,2,0:T(8,128)S(1)} %copy-done.8, f32[1,30,2,20]{1,3,2,0:T(8,128)S(1)} %copy-done.7), kind=kOutput, calls=%fused_computation.25 | convolution fusion | flops 1063899840 | bytes 14755200 | tf_op jit(solution)/shard_map/cdak,fdxyas->fcxyks/dot_general | solution.py:88
  347.0 10.4 %copy.84 = f32[3,2,1,96,20,128]{3,1,0,5,4,2:T(2,128)} copy(f32[3,2,1,96,20,128]{5,4,1,3,0,2:T(8,128)} %fusion.19) | data formatting | bytes 11796480 | tf_op jit(solution)/shard_map/reshape | solution.py:89
  357.4 94.0 %all_to_all.30 = f32[3,2,1,96,2560]{3,1,0,2,4:T(2,128)} all-to-all(f32[3,2,1,96,2560]{3,1,0,2,4:T(2,128)} %bitcast.181), channel_id=1, replica_groups=mesh['row'=8,'col'=4] {'row'}, dimensions={4} | all-to-all | bytes 11796480 | tf_op jit(solution)/shard_map/all_to_all | solution.py:132
  451.4 9.9 %copy.82 = f32[3,2,1,96,8,320]{5,4,3,1,0,2:T(8,128)} copy(f32[3,2,1,96,8,320]{3,1,0,5,4,2:T(2,128)} %bitcast.182) | data formatting | bytes 11796480 | tf_op jit(solution)/shard_map/all_to_all | solution.py:132
  461.2 4.0 fusion.81
  465.3 1.8 slice.103
  468.4 2.6 copy.55
  470.9 2.5 copy.53
  473.5 2.6 copy.56
  476.1 2.5 copy.57
  478.6 2.6 copy.58
  482.4 2.6 copy.60
  485.0 1.9 copy.52
  486.9 3.1 copy.61
  (49 shorter events, 18.4 us)
Async XLA Ops:
  7.2 55.6 %all-gather.3.cloned.1.call-start = ((), (), s32[]{:S(2)}) async-start(), calls=%async_computation.2 | async-start | bytes 2949120 | tf_op jit(solution)/shard_map/all_gather | solution.py:116
  7.9 144.7 %all-gather.5.cloned.1.call-start = ((), (), s32[]{:S(2)}) async-start(), calls=%async_computation.3 | async-start | bytes 5898240 | tf_op jit(solution)/shard_map/all_gather | solution.py:120
  152.6 13.4 %copy-start = (f32[2,2,320,768]{3,2,1,0:T(8,128)S(1)}, f32[2,2,320,768]{3,2,1,0:T(8,128)}, u32[]{:S(2)}) copy-start(f32[2,2,320,768]{3,2,1,0:T(8,128)} %fusion.23) | copy-start | bytes 11796484
  152.6 13.4 %copy-start.2 = (f32[2,768,768]{2,1,0:T(8,128)S(1)}, f32[2,768,768]{2,1,0:T(8,128)}, u32[]{:S(2)}) copy-start(f32[2,768,768]{2,1,0:T(8,128)} %all-gather.5.cloned.1.call-done) | copy-start | bytes 14155780
  188.7 5.0 copy-start.6
  188.7 85.0 %all-to-all-start = ((f32[3,2,1,768,320]{4,1,0,2,3:T(2,128)}), f32[3,2,1,768,320]{4,1,0,2,3:T(2,128)}, u32[]{:S(2)}, u32[]{:S(2)}) async-start(f32[3,2,1,768,320]{4,1,0,2,3:T(2,128)} %copy.41), calls=%async_computation | async-start | bytes 14155776 | tf_op jit(solution)/shard_map/all_to_all | solution.py:127
  308.3 13.7 %copy-start.1 = (f32[96,30,128]{2,0,1:T(8,128)S(1)}, f32[96,30,128]{2,0,1:T(8,128)}, u32[]{:S(2)}) copy-start(f32[96,30,128]{2,0,1:T(8,128)} %copy.47) | copy-start | bytes 4423684
  329.7 5.4 %copy-start.9 = (f32[30,128]{1,0:T(8,128)S(1)}, f32[30,128]{1,0:T(8,128)}, u32[]{:S(2)}) copy-start(f32[30,128]{1,0:T(8,128)} %fusion.69) | copy-start | bytes 46084
  335.0 1.8 copy-start.7
  335.1 1.8 copy-start.8
  485.0 5.0 copy-start.3
  486.9 3.1 copy-start.4
  486.9 3.1 copy-start.5
Sparse Core Ops, SparseCore 0:
  9.6 53.1 all-gather.2
  64.4 88.2 all-gather.4
where the time goes:
time: 506 us; the launch traced here: 500 us
  waiting for transfers between devices  203 us (40%)
  blocking collectives  94 us (19%)
  local copies, waits for them, and re-layouts  88.7 us (18%)
  matrix products  74.6 us (15%)
  other arithmetic  20.4 us (4%)
  between operations  14.8 us (3%)
    all_to_all x1, blocking collectives, shards(): lax.all_to_all(result, 'row', split_axis=4, concat_axis=3, tiled=True)  94 us
    all_gather x1, waiting for transfers between devices, shards(): block_rows = lax.all_gather(back_maps, 'col', axis=1, tiled=True)  76.1 us
    all_to_all x1, waiting for transfers between devices, shards(): lax.all_to_all(fields, 'row', split_axis=3, concat_axis=4, tiled=True)  71.9 us
    all_gather x1, waiting for transfers between devices, shards(): lax.all_gather(forward_map, 'col', axis=0, tiled=True)  53.2 us
    another operation x2, local copies, waits for them, and re-layouts  16.4 us
    dot_general x1, matrix products, shards(): jnp.einsum('fcxkn,jn->fcxkj', sources, lax.all_gather(forward_map, 'col',...  13.7 us
    dot_general x1, matrix products, spanwise_pass(): jnp.einsum('cnds,fdxyas->fcxyan', fine_fwd, data, precision=lax.Precision...  13.7 us
    dot_general x1, matrix products, shards(): jnp.einsum('yj,fcxkj->fcxyk', block_rows[0], coeffs, precision=lax.Precis...  13.3 us
  transfers between devices with their start and end apart: 3, of which 3 were waited for; matrix products, arithmetic and copies ran while one was open for 5% of the time, Pallas kernels for 0%

commit v1 on v0

--- a/solution.py
+++ b/solution.py
@@ -129,7 +129,10 @@
         (1.0 / (1.0 + penalty)).reshape(local_y, 128, count_z // 128), (0, 2, 1)
     )
     result = spanwise_pass(spanwise, factor_grid, count_z)
-    returned = lax.all_to_all(result, "row", split_axis=4, concat_axis=3, tiled=True)
+    size = lax.axis_size("row")
+    blocks = jnp.stack(jnp.split(result, size, axis=4), axis=0)
+    blocks = lax.all_to_all(blocks, "row", split_axis=0, concat_axis=0)
+    returned = jnp.concatenate(blocks, axis=3)
     v_part = returned[1]
     omega_part = form_vorticity(flow_column, span_row, returned[0], returned[2])
     return (jnp.transpose(v_part, (0, 1, 3, 2)), jnp.transpose(omega_part, (0, 1, 3, 2)))

time: 506 us -> 478 us (0.945)
  local copies, waits for them, and re-layouts: 88.7 us -> 74.2 us
  blocking collectives: 94 us -> 82.8 us
    all_to_all x1, blocking collectives: 94 us -> 82.8 us  [shards(): blocks = lax.all_to_all(blocks, 'row', split_axis=0, concat_axis=0)]
    all_to_all x1 -> x0, local copies, waits for them, and re-layouts: 9.87 us -> none  [shards(): lax.all_to_all(result, 'row', split_axis=4, concat_axis=3, tiled=True)]
    split x0 -> x1, local copies, waits for them, and re-layouts: none -> 7.24 us  [shards(): blocks = jnp.stack(jnp.split(result, size, axis=4), axis=0)]
    another operation x2 -> x3, local copies, waits for them, and re-layouts: 16.4 us -> 16.5 us
where the time goes in v1:
time: 478 us; the launch traced here: 472 us
  waiting for transfers between devices  203 us (42%)
  blocking collectives  82.8 us (17%)
  matrix products  74.6 us (16%)
  local copies, waits for them, and re-layouts  74.2 us (16%)
  other arithmetic  18.3 us (4%)
  between operations  14.9 us (3%)
  starting transfers between devices  5.06 us (1%)
    all_to_all x1, blocking collectives, shards(): blocks = lax.all_to_all(blocks, 'row', split_axis=0, concat_axis=0)  82.8 us
    all_gather x1, waiting for transfers between devices, shards(): block_rows = lax.all_gather(back_maps, 'col', axis=1, tiled=True)  76.1 us
    all_to_all x1, waiting for transfers between devices, shards(): lax.all_to_all(fields, 'row', split_axis=3, concat_axis=4, tiled=True)  71.9 us
    all_gather x1, waiting for transfers between devices, shards(): lax.all_gather(forward_map, 'col', axis=0, tiled=True)  53.2 us
    another operation x2, local copies, waits for them, and re-layouts  16.4 us
    dot_general x1, matrix products, shards(): jnp.einsum('fcxkn,jn->fcxkj', sources, lax.all_gather(forward_map, 'col',...  13.7 us
    dot_general x1, matrix products, spanwise_pass(): jnp.einsum('cnds,fdxyas->fcxyan', fine_fwd, data, precision=lax.Precision...  13.7 us
    dot_general x1, matrix products, shards(): jnp.einsum('yj,fcxkj->fcxyk', block_rows[0], coeffs, precision=lax.Precis...  13.3 us
  transfers between devices with their start and end apart: 3, of which 3 were waited for; matrix products, arithmetic and copies ran while one was open for 5% of the time, Pallas kernels for 0%

profile of v1, /device:TPU:0, one launch (start us, length us, event | category | flops | bytes accessed | tf_op | source)
XLA Modules:
  0.0 472.4 jit_solution(1457501060607295183)
XLA Ops:
  9.6 53.2 %all-gather.3.cloned.1.call-done = f32[768,768]{1,0:T(8,128)} async-done(((f32[192,768]{1,0:T(8,128)}), f32[768,768]{1,0:T(8,128)}) %all-gather.3.cloned.1.call-update) | async-done | bytes 2359312 | tf_op jit(solution)/shard_map/all_gather | solution.py:116
  62.8 13.7 %fusion.23 = f32[2,2,320,768]{3,2,1,0:T(8,128)} fusion(f32[768,768]{1,0:T(8,128)} %all-gather.3.cloned.1.call-done, f32[1,2,1,320,768]{4,3,1,0,2:T(8,128)} %bitcast.224, f32[1,2,1,320,768]{4,3,1,0,2:T(8,128)} %bitcast.225, f32[320,768]{1,0:T(8,128)S(1)} %add_divide_fusion.2), kind=kOutput, calls=%fused_computation.31 | convolution fusion | flops 9061662720 | bytes 11206656 | tf_op jit(solution)/shard_map/fcxkn,jn->fcxkj/dot_general | solution.py:113
  76.5 76.1 %all-gather.5.cloned.1.call-done = f32[2,768,768]{2,1,0:T(8,128)} async-done(((f32[2,192,768]{2,1,0:T(8,128)}), f32[2,768,768]{2,1,0:T(8,128)}) %all-gather.5.cloned.1.call-update) | async-done | bytes 4718608 | tf_op jit(solution)/shard_map/all_gather | solution.py:120
  152.6 13.3 %fusion.21 = f32[2,2,320,768]{3,2,1,0:T(8,128)S(1)} fusion(f32[2,2,320,768]{3,2,1,0:T(8,128)} %fusion.23, f32[2,768,768]{2,1,0:T(8,128)} %all-gather.5.cloned.1.call-done), kind=kOutput, calls=%fused_computation.29 | convolution fusion | flops 9059696640 | bytes 10223616 | tf_op jit(solution)/shard_map/yj,fcxkj->fcxyk/dot_general | solution.py:121
  166.0 5.5 %fusion.26 = f32[2,1,768,320]{2,3,0,1:T(8,128)S(1)} fusion(f32[2,768,768]{2,1,0:T(8,128)S(1)} %copy-done.2, f32[2,2,320,768]{3,2,1,0:T(8,128)S(1)} %copy-done), kind=kOutput, calls=%fused_computation.36 | convolution fusion | flops 4529848320 | bytes 6291456 | tf_op jit(solution)/shard_map/yj,cxkj->cxyk/dot_general | solution.py:122
  172.5 3.0 pad_maximum_fusion
  175.5 13.2 %copy.45 = f32[3,2,1,768,320]{4,1,0,2,3:T(2,128)} copy(f32[3,2,1,768,320]{3,4,1,0,2:T(8,128)} %pad_maximum_fusion) | data formatting | bytes 11796480 | tf_op jit(solution)/shard_map/stack | solution.py:126
  188.7 5.0 %all-to-all-start = ((f32[3,2,1,768,320]{4,1,0,2,3:T(2,128)}), f32[3,2,1,768,320]{4,1,0,2,3:T(2,128)}, u32[]{:S(2)}, u32[]{:S(2)}) async-start(f32[3,2,1,768,320]{4,1,0,2,3:T(2,128)} %copy.45), calls=%async_computation | async-start | bytes 14155776 | tf_op jit(solution)/shard_map/all_to_all | solution.py:127
  193.9 1.8 copy.50
  195.6 1.6 reshape.761
  197.2 1.8 copy.51
  201.8 71.9 %all-to-all-done = f32[3,2,1,768,320]{4,1,0,2,3:T(2,128)} async-done(((f32[3,2,1,768,320]{4,1,0,2,3:T(2,128)}), f32[3,2,1,768,320]{4,1,0,2,3:T(2,128)}, u32[]{:S(2)}, u32[]{:S(2)}) %all-to-all-start) | async-done | bytes 5898272 | tf_op jit(solution)/shard_map/all_to_all | solution.py:127
  273.7 3.5 copy.46
  277.2 7.0 %copy.75 = f32[3,2,1,96,8,320]{5,4,1,3,0,2:T(8,128)} copy(f32[3,2,1,96,8,320]{5,3,4,1,0,2:T(8,128)S(1)} %bitcast.215) | data formatting | bytes 11796480 | tf_op jit(solution)/shard_map/reshape.29
  284.1 9.5 %reshape.769 = f32[3,2,96,20,128,1]{4,3,1,2,0,5:T(8,128)} reshape(f32[3,2,1,96,8,320]{5,4,1,3,0,2:T(8,128)} %copy.75) | data formatting | bytes 11796480 | tf_op jit(solution)/shard_map/reshape.29
  293.6 10.7 %fusion.13 = f32[3,2,1,96,30,128]{5,4,1,3,0,2:T(8,128)S(1)} fusion(f32[3,2,96,20,128,1]{4,3,1,2,0,5:T(8,128)} %reshape.769, f32[1,30,2,20]{1,3,2,0:T(8,128)S(1)} %get-tuple-element.35, f32[1,30,2,20]{1,3,2,0:T(8,128)S(1)} %get-tuple-element.38), kind=kOutput, calls=%fused_computation.23 | convolution fusion | flops 1061685632 | bytes 14755200 | tf_op jit(solution)/shard_map/cadk,fdxyks->fcxyas/dot_general | solution.py:82
  304.3 2.5 multiply_subtract_fusion.1
  306.8 1.6 maximum_bitcast_fusion
  308.3 13.7 %fusion.5 = f32[3,96,30,2,128,1]{4,1,5,3,2,0:T(8,128)S(1)} fusion(f32[3,2,96,30,128,1]{4,3,1,2,0,5:T(8,128)S(1)} %maximum_bitcast_fusion, f32[1,128,2,128]{3,1,2,0:T(8,128)S(1)} %get-tuple-element.29, f32[1,128,2,128]{3,1,2,0:T(8,128)S(1)} %get-tuple-element.32), kind=kOutput, calls=%fused_computation.9 | convolution fusion | flops 6794838016 | bytes 17956864 | tf_op jit(solution)/shard_map/cnds,fdxyas->fcxyan/dot_general | solution.py:84
  322.1 7.6 %fusion.16 = f32[3,96,30,2,128]{4,1,3,2,0:T(8,128)S(1)} fusion(f32[3,96,30,2,128,1]{4,1,5,3,2,0:T(8,128)S(1)} %fusion.5, f32[96,30,128]{2,0,1:T(8,128)S(1)} %copy-done.1, f32[1,128,2,128]{3,1,2,0:T(8,128)S(1)} %get-tuple-element.33, f32[1,128,2,128]{3,1,2,0:T(8,128)S(1)} %get-tuple-element.28), kind=kOutput, calls=%fused_computation.24 | convolution fusion | flops 6797049856 | bytes 19431424 | tf_op jit(solution)/shard_map/ckdn,fdxyan->fcxyak/dot_general | solution.py:86
  329.7 5.4 %copy.115 = f32[3,96,30,2,128]{4,2,3,1,0:T(8,128)S(1)} copy(f32[3,96,30,2,128]{4,1,3,2,0:T(8,128)S(1)} %fusion.16) | data formatting | bytes 17694720 | tf_op jit(solution)/shard_map/ckdn,fdxyan->fcxyak/dot_general | solution.py:86
  335.1 1.8 multiply_subtract_fusion
  336.9 10.1 %fusion.19 = f32[3,2,1,96,20,128]{5,4,1,3,0,2:T(8,128)} fusion(f32[3,1,1,96,30,128]{5,4,1,3,0,2:T(8,128)S(1)} %get-tuple-element.9, f32[3,1,1,96,30,128]{5,4,1,3,0,2:T(8,128)S(1)} %get-tuple-element.8, f32[1,30,2,20]{1,3,2,0:T(8,128)S(1)} %copy-done.8, f32[1,30,2,20]{1,3,2,0:T(8,128)S(1)} %copy-done.7), kind=kOutput, calls=%fused_computation.25 | convolution fusion | flops 1063899840 | bytes 14755200 | tf_op jit(solution)/shard_map/cdak,fdxyas->fcxyks/dot_general | solution.py:88
  347.0 8.7 %reshape.783 = f32[3,2,1,96,2560]{4,1,3,0,2:T(2,128)} reshape(f32[3,2,1,96,20,128]{5,4,1,3,0,2:T(8,128)} %fusion.19) | data formatting | bytes 11796480 | tf_op jit(solution)/shard_map/reshape | solution.py:89
  355.7 7.2 %fusion.90 = (f32[3,2,1,96,320]{4,1,3,0,2:T(2,128)S(1)}, f32[3,2,1,96,320]{4,1,3,0,2:T(2,128)S(1)}, f32[3,2,1,96,320]{4,1,3,0,2:T(2,128)S(1)}, f32[3,2,1,96,320]...) fusion(f32[3,2,1,96,2560]{4,1,3,0,2:T(2,128)} %reshape.783), kind=kLoop, calls=%fused_computation.142 | loop fusion | bytes 11796480 | tf_op jit(solution)/shard_map/split | solution.py:133
  363.5 82.8 %all_to_all.20 = f32[8,3,2,1,96,320]{5,4,2,1,3,0:T(8,128)S(1)} all-to-all(f32[8,3,2,1,96,320]{5,4,2,1,3,0:T(8,128)S(1)} %fusion.27), channel_id=1, replica_groups=mesh['row'=8,'col'=4] {'row'}, dimensions={0} | all-to-all | bytes 11796480 | tf_op jit(solution)/shard_map/all_to_all | solution.py:134
  446.3 1.9 fusion.89
  448.5 2.6 copy.55
  451.0 2.6 copy.56
  453.6 2.6 copy.57
  457.5 1.6 copy.54
  459.1 3.1 copy.59
  (53 shorter events, 11.3 us)
Async XLA Ops:
  7.2 55.6 %all-gather.3.cloned.1.call-start = ((), (), s32[]{:S(2)}) async-start(), calls=%async_computation.2 | async-start | bytes 2949120 | tf_op jit(solution)/shard_map/all_gather | solution.py:116
  7.9 144.7 %all-gather.5.cloned.1.call-start = ((), (), s32[]{:S(2)}) async-start(), calls=%async_computation.3 | async-start | bytes 5898240 | tf_op jit(solution)/shard_map/all_gather | solution.py:120
  152.6 13.4 %copy-start = (f32[2,2,320,768]{3,2,1,0:T(8,128)S(1)}, f32[2,2,320,768]{3,2,1,0:T(8,128)}, u32[]{:S(2)}) copy-start(f32[2,2,320,768]{3,2,1,0:T(8,128)} %fusion.23) | copy-start | bytes 11796484
  152.6 13.4 %copy-start.2 = (f32[2,768,768]{2,1,0:T(8,128)S(1)}, f32[2,768,768]{2,1,0:T(8,128)}, u32[]{:S(2)}) copy-start(f32[2,768,768]{2,1,0:T(8,128)} %all-gather.5.cloned.1.call-done) | copy-start | bytes 14155780
  188.7 5.0 %copy-start.6 = (f32[96,3840]{1,0:T(8,128)S(1)}, f32[96,3840]{1,0:T(8,128)}, u32[]{:S(2)}) copy-start(f32[96,3840]{1,0:T(8,128)} %param.11) | copy-start | bytes 4423684
  188.7 85.0 %all-to-all-start = ((f32[3,2,1,768,320]{4,1,0,2,3:T(2,128)}), f32[3,2,1,768,320]{4,1,0,2,3:T(2,128)}, u32[]{:S(2)}, u32[]{:S(2)}) async-start(f32[3,2,1,768,320]{4,1,0,2,3:T(2,128)} %copy.45), calls=%async_computation | async-start | bytes 14155776 | tf_op jit(solution)/shard_map/all_to_all | solution.py:127
  308.3 13.7 %copy-start.1 = (f32[96,30,128]{2,0,1:T(8,128)S(1)}, f32[96,30,128]{2,0,1:T(8,128)}, u32[]{:S(2)}) copy-start(f32[96,30,128]{2,0,1:T(8,128)} %copy.51) | copy-start | bytes 4423684
  329.7 5.4 %copy-start.9 = (f32[30,128]{1,0:T(8,128)S(1)}, f32[30,128]{1,0:T(8,128)}, u32[]{:S(2)}) copy-start(f32[30,128]{1,0:T(8,128)} %fusion.77) | copy-start | bytes 46084
  335.1 1.8 copy-start.7
  335.1 1.8 copy-start.8
  457.5 4.7 copy-start.3
  459.1 3.1 copy-start.4
  459.1 3.1 copy-start.5
Sparse Core Ops, SparseCore 0:
  9.6 53.1 all-gather.2
  64.4 88.2 all-gather.4
